TPU v7x, 32 devices: a whole 2x2x4 slice. The times are simulated.
32 devices in a mesh: dp: 4 (over z), mp: 8 (over y, x, core).
Axes of the slice: x: 2, y: 2, z: 4, core: 2. Of those that a mesh axis runs over, the one named last changes fastest.
Arguments:
- old_weight: float32 [768, 43008], P('dp', 'mp'), may hold values from -6 to 6
- old_first: float32 [768, 43008], P('dp', 'mp'), may hold values from -6 to 6
- old_second: float32 [768, 43008], P('dp', 'mp'), may hold values from 0.1 to 2
- gradient: float32 [768, 43008], P('dp', 'mp'), may hold values from -6 to 6
- old_rows: int32 [4, 192], replicated, may hold values from 0 to 767, as said below
- new_rows: int32 [4, 192], replicated, may hold values from 0 to 767, as said below
- new_units: int32 [8, 42], replicated, may hold values from 0 to 335, as said below
- step: int32 [1], replicated, may hold values from 1 to 49
Outputs:
- new_weight: float32 [768, 43008], P('dp', 'mp')
- new_first: float32 [768, 43008], P('dp', 'mp')
- new_second: float32 [768, 43008], P('dp', 'mp')
- update: float32 [768, 43008], P('dp', 'mp')
Inputs may be any that keep to these rules, and one draw needn't show every extreme that they name: old_rows names every slab row once. Of the rows in one old data shard, at most 72 are named by any one new data shard, and in every draw each old data shard has exactly 72 for some new data shard. new_rows names every slab row once; the bound on rows from one old data shard to one new data shard, stated for old_rows, holds. new_units names every column unit once. Of the units u * 42 to u * 42 + 41 of old tensor shard u, at most 8 are named by any one new tensor shard, and in every draw each old tensor shard has exactly 8 for some new tensor shard.
All inputs are finite; a program needn't handle non-finite values.
Results may differ from a plain program's by a relative error of at most 0.00018.
Values sent between devices are 32-bit elements; how exact they have to be, the bound alone decides.
A program may use at most 128 MiB of HBM per device.

v0:
```python
import jax
import jax.numpy as jnp
from jax import lax
from jax.sharding import PartitionSpec as P

HEAD_DIM = 128


beta_one = 0.9
beta_two = 0.999
epsilon = 1e-08
learn_rate = 0.001
decay_rate = 0.1


def adam_step(weight, first, second, gradient, step):
    step_count = step[0].astype(jnp.float32)
    new_first = beta_one * first + (1.0 - beta_one) * gradient
    new_second = beta_two * second + (1.0 - beta_two) * gradient * gradient
    first_fix = 1.0 - jnp.power(jnp.float32(beta_one), step_count)
    second_fix = 1.0 - jnp.power(jnp.float32(beta_two), step_count)
    update = (
        new_first / first_fix / (jnp.sqrt(new_second / second_fix) + epsilon) + decay_rate * weight
    )
    new_weight = weight - learn_rate * update
    return (new_weight, new_first, new_second, update)


def moving_plan(old_flat, new_flat, shards, per_shard):
    total_rows = shards * per_shard
    new_place = jnp.argsort(new_flat, stable=True)
    old_place = jnp.argsort(old_flat, stable=True)
    target = new_place[old_flat] // per_shard
    onehot = (target[:, None] == jnp.arange(shards, dtype=jnp.int32)[None, :]).astype(jnp.int32)
    onehot = onehot.reshape(shards, per_shard, shards)
    before = jnp.cumsum(onehot, axis=1) - onehot
    slot_rank = jnp.sum(before * onehot, axis=2).reshape(total_rows)
    return (target, slot_rank, old_place)


def send_index(target, slot_rank, owner, shards, per_shard, capacity):
    mine_target = lax.dynamic_slice_in_dim(target, owner * per_shard, per_shard)
    mine_rank = lax.dynamic_slice_in_dim(slot_rank, owner * per_shard, per_shard)
    spots = mine_target * capacity + mine_rank
    slots = jnp.arange(shards * capacity, dtype=jnp.int32)
    match = (slots[:, None] == spots[None, :]).astype(jnp.int32)
    sources = jnp.arange(per_shard, dtype=jnp.int32)[None, :]
    found = jnp.sum(match, axis=1)
    return jnp.sum(match * sources, axis=1) + per_shard * (1 - found)


def receive_index(new_flat, slot_rank, old_place, owner, per_shard, capacity):
    wanted = lax.dynamic_slice_in_dim(new_flat, owner * per_shard, per_shard)
    anchor = old_place[wanted]
    return anchor // per_shard * capacity + slot_rank[anchor]


def room_for(count, shards):
    share = count // shards
    return share + share // 2 + min(count % shards, 1)


def body(old_weight, old_first, old_second, gradient, old_rows, new_rows, new_units, step):
    dp_shards = lax.axis_size("dp")
    mp_shards = lax.axis_size("mp")
    dp_index = lax.axis_index("dp")
    mp_index = lax.axis_index("mp")
    row_count = old_weight.shape[0]
    unit_count = new_units.shape[1]
    unit_width = HEAD_DIM
    row_room = room_for(row_count, dp_shards)
    unit_room = room_for(unit_count, mp_shards)
    old_flat = old_rows.reshape(-1)
    new_flat = new_rows.reshape(-1)
    row_target, row_rank, row_place = moving_plan(old_flat, new_flat, dp_shards, row_count)
    row_send = send_index(row_target, row_rank, dp_index, dp_shards, row_count, row_room)
    row_take = receive_index(new_flat, row_rank, row_place, dp_index, row_count, row_room)
    unit_old = jnp.arange(mp_shards * unit_count, dtype=jnp.int32)
    unit_flat = new_units.reshape(-1)
    unit_target, unit_rank, unit_place = moving_plan(unit_old, unit_flat, mp_shards, unit_count)
    unit_send = send_index(unit_target, unit_rank, mp_index, mp_shards, unit_count, unit_room)
    unit_take = receive_index(unit_flat, unit_rank, unit_place, mp_index, unit_count, unit_room)
    states = (old_weight, old_first, old_second)
    packed = tuple(
        (
            jnp.take(moment, row_send, axis=0, mode="fill", fill_value=0).reshape(
                dp_shards, row_room, unit_count * unit_width
            )
            for moment in states
        )
    )
    arrived = (
        lax.all_to_all(packed[0], "dp", split_axis=0, concat_axis=0, tiled=True),
        lax.all_to_all(packed[1], "dp", split_axis=0, concat_axis=0, tiled=True),
        lax.all_to_all(packed[2], "dp", split_axis=0, concat_axis=0, tiled=True),
    )
    rowed = tuple(
        (
            jnp.take(
                moment.reshape(dp_shards * row_room, unit_count * unit_width), row_take, axis=0
            )
            for moment in arrived
        )
    )
    packed = tuple(
        (
            jnp.take(
                moment.reshape(row_count, unit_count, unit_width),
                unit_send,
                axis=1,
                mode="fill",
                fill_value=0,
            ).reshape(row_count, mp_shards, unit_room, unit_width)
            for moment in rowed
        )
    )
    arrived = (
        lax.all_to_all(packed[0], "mp", split_axis=1, concat_axis=1, tiled=True),
        lax.all_to_all(packed[1], "mp", split_axis=1, concat_axis=1, tiled=True),
        lax.all_to_all(packed[2], "mp", split_axis=1, concat_axis=1, tiled=True),
    )
    placed = tuple(
        (
            jnp.take(
                moment.reshape(row_count, mp_shards * unit_room, unit_width), unit_take, axis=1
            ).reshape(row_count, unit_count * unit_width)
            for moment in arrived
        )
    )
    return adam_step(placed[0], placed[1], placed[2], gradient, step)


def solution(mesh):
    return jax.shard_map(
        body,
        mesh=mesh,
        in_specs=(P("dp", "mp"), P("dp", "mp"), P("dp", "mp"), P("dp", "mp"), P(), P(), P(), P()),
        out_specs=(P("dp", "mp"), P("dp", "mp"), P("dp", "mp"), P("dp", "mp")),
        check_vma=False,
    )
```

profile of v0, /device:TPU:9, one launch (start us, length us, event | category | flops | bytes accessed | tf_op | source)
XLA Modules:
  0.0 778.8 jit_solution(11781780258219444977)
XLA Ops:
  15.7 11.9 %gather_fusion.14 = f32[288,5376]{1,0:T(8,128)} fusion(f32[192,5376]{1,0:T(8,128)} %param.18, s32[1024]{0:T(1024)S(1)} %pad_clamp_fusion.3), kind=kCustom, calls=%fused_computation.5.clone | custom fusion | bytes 12387456 | tf_op jit(solution)/shard_map/jit(_take)/gather | solution.py:86
  27.6 11.9 %gather_fusion.10 = f32[288,5376]{1,0:T(8,128)} fusion(f32[192,5376]{1,0:T(8,128)} %param.17, s32[1024]{0:T(1024)S(1)} %pad_clamp_fusion.3), kind=kCustom, calls=%fused_computation.4.clone | custom fusion | bytes 12387456 | tf_op jit(solution)/shard_map/jit(_take)/gather | solution.py:86
  39.5 12.0 %gather_fusion.6 = f32[288,5376]{1,0:T(8,128)} fusion(f32[192,5376]{1,0:T(8,128)} %param.16, s32[1024]{0:T(1024)S(1)} %pad_clamp_fusion.3), kind=kCustom, calls=%fused_computation.clone | custom fusion | bytes 12387456 | tf_op jit(solution)/shard_map/jit(_take)/gather | solution.py:86
  51.5 9.9 %broadcast_select_fusion.4 = (f32[288,5376]{1,0:T(8,128)S(1)}, f32[288,5376]{1,0:T(8,128)S(1)}, f32[288,5376]{1,0:T(8,128)}) fusion(f32[288,5376]{1,0:T(8,128)} %gather_fusion.10, pred[288]{0:T(512)(128)(4,1)S(1)} %get-tuple-element.32, f32[288,5376]{1,0:T(8,128)} %gather_fusion.14, f32[288,5376]{1,0:T(8,128)} %gather_fusion.6), kind=kLoop, calls=%fused_computation.39 | loop fusion | flops 4644864 | bytes 37159200 | tf_op jit(solution)/shard_map/jit(_take)/select_n | solution.py:86
  61.4 138.7 %all_to_all.30 = f32[4,72,5376]{2,1,0:T(8,128)} all-to-all(f32[4,72,5376]{2,1,0:T(8,128)S(1)} %bitcast.83), channel_id=1, replica_groups=mesh['dp'=4,'mp'=8] {'dp'}, dimensions={0} | all-to-all | bytes 12386304 | tf_op jit(solution)/shard_map/all_to_all | solution.py:95
  200.1 139.1 %all_to_all.31 = f32[4,72,5376]{2,1,0:T(8,128)} all-to-all(f32[4,72,5376]{2,1,0:T(8,128)S(1)} %bitcast.82), channel_id=1, replica_groups=mesh['dp'=4,'mp'=8] {'dp'}, dimensions={0} | all-to-all | bytes 12386304 | tf_op jit(solution)/shard_map/all_to_all | solution.py:94
  339.2 6.4 all-to-all-start
  361.0 8.4 %gather_fusion.15 = f32[192,5376]{1,0:T(8,128)} fusion(f32[288,5376]{1,0:T(8,128)} %bitcast.73, s32[1024]{0:T(1024)S(1)} %pad_clamp_fusion.2), kind=kCustom, calls=%fused_computation.7.clone | custom fusion | bytes 8258304 | tf_op jit(solution)/shard_map/jit(_take)/gather | solution.py:99
  369.3 8.4 %gather_fusion.11 = f32[192,5376]{1,0:T(8,128)} fusion(f32[288,5376]{1,0:T(8,128)} %bitcast.74, s32[1024]{0:T(1024)S(1)} %pad_clamp_fusion.2), kind=kCustom, calls=%fused_computation.6.clone | custom fusion | bytes 8258304 | tf_op jit(solution)/shard_map/jit(_take)/gather | solution.py:99
  377.7 98.9 %all-to-all-done = f32[4,72,5376]{2,1,0:T(8,128)} async-done(((f32[4,72,5376]{2,1,0:T(8,128)}), f32[4,72,5376]{2,1,0:T(8,128)}, u32[]{:S(2)}, u32[]{:S(2)}) %all-to-all-start) | async-done | bytes 6193184 | tf_op jit(solution)/shard_map/all_to_all | solution.py:93
  476.6 8.4 %gather_fusion.7 = f32[192,5376]{1,0:T(8,128)} fusion(f32[288,5376]{1,0:T(8,128)} %bitcast.7, s32[1024]{0:T(1024)S(1)} %pad_clamp_fusion.2), kind=kCustom, calls=%fused_computation.1.clone | custom fusion | bytes 8258304 | tf_op jit(solution)/shard_map/jit(_take)/gather | solution.py:99
  485.0 9.7 %select_bitcast_fusion.1 = (f32[24,42,8,128]{3,2,1,0:T(8,128)}, f32[24,42,8,128]{3,2,1,0:T(8,128)}, f32[24,42,8,128]{3,2,1,0:T(8,128)}) fusion(f32[192,5376]{1,0:T(8,128)} %gather_fusion.11, pred[192]{0:T(512)(128)(4,1)S(1)} %get-tuple-element.30, f32[192,5376]{1,0:T(8,128)} %gather_fusion.15, f32[192,5376]{1,0:T(8,128)} %gather_fusion.7), kind=kLoop, calls=%fused_computation.32 | loop fusion | flops 3096576 | bytes 24772800
  502.2 5.7 gather_fusion.12
  507.9 5.8 gather_fusion.16
  518.4 5.8 gather_fusion.8
  524.2 10.3 %broadcast_select_fusion.1 = (f32[64,192,128]{2,1,0:T(8,128)S(1)}, f32[64,192,128]{2,1,0:T(8,128)S(1)}, f32[64,192,128]{2,1,0:T(8,128)}) fusion(f32[64,192,128]{2,1,0:T(8,128)} %gather_fusion.12, pred[64]{0:T(512)(128)(4,1)S(1)} %get-tuple-element.26, f32[64,192,128]{2,1,0:T(8,128)} %gather_fusion.16, f32[64,192,128]{2,1,0:T(8,128)} %gather_fusion.8), kind=kLoop, calls=%fused_computation.36 | loop fusion | flops 4718592 | bytes 37748800 | tf_op jit(solution)/shard_map/jit(_take)/select_n | solution.py:107
  534.5 76.8 %all_to_all.32 = f32[192,8,8,128]{3,0,2,1:T(8,128)} all-to-all(f32[192,8,8,128]{3,0,2,1:T(8,128)S(1)} %bitcast.80), channel_id=1, replica_groups=mesh['dp'=4,'mp'=8] {'mp'}, dimensions={1} | all-to-all | bytes 12582912 | tf_op jit(solution)/shard_map/all_to_all | solution.py:120
  611.2 74.9 %all_to_all.33 = f32[192,8,8,128]{3,0,2,1:T(8,128)} all-to-all(f32[192,8,8,128]{3,0,2,1:T(8,128)S(1)} %bitcast.79), channel_id=1, replica_groups=mesh['dp'=4,'mp'=8] {'mp'}, dimensions={1} | all-to-all | bytes 12582912 | tf_op jit(solution)/shard_map/all_to_all | solution.py:119
  686.1 5.9 all-to-all-start.1
  698.1 5.6 gather_fusion.17
  703.7 5.6 gather_fusion.13
  709.3 50.8 %all-to-all-done.1 = f32[192,8,8,128]{3,0,2,1:T(8,128)} async-done(((f32[192,8,8,128]{3,0,2,1:T(8,128)}), f32[192,8,8,128]{3,0,2,1:T(8,128)}, u32[]{:S(2)}, u32[]{:S(2)}) %all-to-all-start.1) | async-done | bytes 6291488 | tf_op jit(solution)/shard_map/all_to_all | solution.py:118
  760.1 5.6 gather_fusion.9
  771.6 6.8 bitcast_subtract_fusion
  (79 shorter events, 53.7 us)
Async XLA Ops:
  339.2 6.4 copy-start.3
  339.2 6.5 copy-start.4
  339.2 137.4 %all-to-all-start = ((f32[4,72,5376]{2,1,0:T(8,128)}), f32[4,72,5376]{2,1,0:T(8,128)}, u32[]{:S(2)}, u32[]{:S(2)}) async-start(f32[4,72,5376]{2,1,0:T(8,128)} %bitcast.81), calls=%async_computation | async-start | bytes 12386304 | tf_op jit(solution)/shard_map/all_to_all | solution.py:93
  494.6 4.8 copy-start.1
  686.1 74.0 %all-to-all-start.1 = ((f32[192,8,8,128]{3,0,2,1:T(8,128)}), f32[192,8,8,128]{3,0,2,1:T(8,128)}, u32[]{:S(2)}, u32[]{:S(2)}) async-start(f32[192,8,8,128]{3,0,2,1:T(8,128)} %bitcast.78), calls=%async_computation.1 | async-start | bytes 12582912 | tf_op jit(solution)/shard_map/all_to_all | solution.py:118
  765.7 4.7 copy-start
  765.7 5.8 copy-start.2
where the time goes:
time: 794 us; the launch traced here: 779 us
  blocking collectives  429 us (54%)
  waiting for transfers between devices  150 us (19%)
  local copies, waits for them, and re-layouts  121 us (15%)
  other arithmetic  64.1 us (8%)
  starting transfers between devices  12.3 us (2%)
    all_to_all x1, blocking collectives, body(): lax.all_to_all(packed[1], 'dp', split_axis=0, concat_axis=0, tiled=True)  139 us
    all_to_all x1, blocking collectives, body(): lax.all_to_all(packed[2], 'dp', split_axis=0, concat_axis=0, tiled=True)  139 us
    all_to_all x1, waiting for transfers between devices, body(): lax.all_to_all(packed[0], 'dp', split_axis=0, concat_axis=0, tiled=True)  98.9 us
    all_to_all x1, blocking collectives, body(): lax.all_to_all(packed[2], 'mp', split_axis=1, concat_axis=1, tiled=True)  76.8 us
    all_to_all x1, blocking collectives, body(): lax.all_to_all(packed[1], 'mp', split_axis=1, concat_axis=1, tiled=True)  74.9 us
    all_to_all x1, waiting for transfers between devices, body(): lax.all_to_all(packed[0], 'mp', split_axis=1, concat_axis=1, tiled=True)  50.8 us
    gather x3, local copies, waits for them, and re-layouts, body(): jnp.take(moment, row_send, axis=0, mode='fill', fill_value=0)  35.8 us
    gather x3, local copies, waits for them, and re-layouts, body(): jnp.take(moment.reshape(dp_shards * row_room, unit_count * unit_width), r...  25.1 us
  transfers between devices with their start and end apart: 2, of which 2 were waited for; matrix products, arithmetic and copies ran while one was open for 6% of the time, Pallas kernels for 0%

commit v1 on v0

v1 whole, which is shorter than its diff:
```python
import functools
import jax
import jax.numpy as jnp
from jax import lax
from jax.experimental import pallas as pl
from jax.experimental.pallas import tpu as pltpu
from jax.sharding import PartitionSpec as P

UNIT = 128
MESH = pl.DeviceIdType.MESH

beta_one = 0.9
beta_two = 0.999
epsilon = 1e-08
learn_rate = 0.001
decay_rate = 0.1


def room_for(count, shards):
    share = count // shards
    return share + share // 2 + min(count % shards, 1)


def iota(n):
    return jnp.arange(n, dtype=jnp.int32)


def row_plan(old_rows, new_rows, dp_index, room):
    shards, per = old_rows.shape
    old_flat = old_rows.reshape(-1)
    new_flat = new_rows.reshape(-1)
    total = shards * per
    same = (old_flat[:, None] == new_flat[None, :]).astype(jnp.int32)
    target = jnp.sum(same * (iota(total) // per)[None, :], axis=1).reshape(shards, per)
    earlier = (iota(per)[:, None] > iota(per)[None, :])[None]
    rank = jnp.sum(((target[:, :, None] == target[:, None, :]) & earlier).astype(jnp.int32), axis=2)
    my_target = lax.dynamic_index_in_dim(target, dp_index, 0, False)
    my_rank = lax.dynamic_index_in_dim(rank, dp_index, 0, False)
    shift = lax.rem(my_target - dp_index + shards, shards)
    spot = shift * room + my_rank
    pack = (iota(shards * room)[:, None] == spot[None, :]).astype(jnp.bfloat16)
    wanted = lax.dynamic_index_in_dim(new_rows, dp_index, 0, False)
    anchor = (iota(total) // per) * room + rank.reshape(-1)
    found = (wanted[:, None] == old_flat[None, :]).astype(jnp.int32)
    column = jnp.sum(found * anchor[None, :], axis=1)
    take = (column[:, None] == iota(shards * room)[None, :]).astype(jnp.bfloat16)
    return pack, take


def unit_plan(new_units, mp_index, chunks):
    shards, per = new_units.shape
    total = shards * per
    unit_flat = new_units.reshape(-1)
    same = (iota(total)[:, None] == unit_flat[None, :]).astype(jnp.int32)
    target = jnp.sum(same * (iota(total) // per)[None, :], axis=1).reshape(shards, per)
    ahead = (target[:, None, :] < target[:, :, None]) | (
        (target[:, None, :] == target[:, :, None])
        & (iota(per)[None, None, :] < iota(per)[None, :, None])
    )
    place = jnp.sum(ahead.astype(jnp.int32), axis=2)
    my_place = lax.dynamic_index_in_dim(place, mp_index, 0, False)
    my_target = lax.dynamic_index_in_dim(target, mp_index, 0, False)
    deep = -(-per // chunks)
    at = (iota(deep)[None, :] * chunks + iota(chunks)[:, None]).reshape(-1)
    order = jnp.sum((at[:, None] == my_place[None, :]).astype(jnp.int32) * iota(per)[None, :], axis=1)
    lane = my_place % chunks * shards + my_target
    slots = iota(chunks * shards)
    chosen = jnp.sum(
        (slots[:, None] == lane[None, :]).astype(jnp.int32) * (my_place // chunks)[None, :], axis=1
    )
    wanted = lax.dynamic_index_in_dim(new_units, mp_index, 0, False)
    arrive = (place % chunks * shards + iota(shards)[:, None]).reshape(-1)
    found = (wanted[:, None] == iota(total)[None, :]).astype(jnp.int32)
    landed = jnp.sum(found * arrive[None, :], axis=1)
    return order, chosen, landed


def exact_dot(onehot, values):
    width = values.shape[1]
    high = values.astype(jnp.bfloat16)
    rest = values - high.astype(jnp.float32)
    middle = rest.astype(jnp.bfloat16)
    low = (rest - middle.astype(jnp.float32)).astype(jnp.bfloat16)
    parts = jnp.concatenate([high, middle, low], axis=1)
    out = jnp.dot(onehot, parts, preferred_element_type=jnp.float32)
    return (out[:, :width] + out[:, width : 2 * width]) + out[:, 2 * width :]


def move_kernel(dp, mp, rows, units, room, chunks, *refs):
    order_ref, chosen_ref, pack_ref, take_ref = refs[:4]
    states = refs[4:7]
    out_ref = refs[7]
    scratch = refs[8:]
    arrive = scratch[:chunks]
    (held, leave, unit_leave, load_sem, row_send, row_recv, unit_send, unit_recv, own_sem) = scratch[
        chunks:
    ]
    me_dp = lax.axis_index("dp")
    me_mp = lax.axis_index("mp")
    deep = -(-units // chunks)

    def load(u, carry):
        for a in range(3):
            pltpu.make_async_copy(
                states[a].at[:, pl.ds(pl.multiple_of(u * UNIT, UNIT), UNIT)],
                held.at[a, u],
                load_sem.at[a],
            ).start()
        return carry

    lax.fori_loop(0, units, load, 0)
    barrier = pltpu.get_barrier_semaphore()
    for k in range(1, dp):
        pl.semaphore_signal(
            barrier, inc=1, device_id=(lax.rem(me_dp + k, dp), me_mp), device_id_type=MESH
        )
    for k in range(1, mp):
        pl.semaphore_signal(
            barrier, inc=1, device_id=(me_dp, lax.rem(me_mp + k, mp)), device_id_type=MESH
        )
    pl.semaphore_wait(barrier, dp + mp - 2)

    def count(j):
        return -(-(units - j) // chunks)

    def row_copy(j, k):
        n = count(j)
        return pltpu.make_async_remote_copy(
            src_ref=leave.at[j % 2, k - 1, pl.ds(0, n)],
            dst_ref=arrive[j].at[pl.ds(0, n), :, pl.ds(pl.multiple_of(me_dp * room, 8), room), :],
            send_sem=row_send.at[j % 2, k - 1],
            recv_sem=row_recv.at[j, k - 1],
            device_id=(lax.rem(me_dp + k, dp), me_mp),
            device_id_type=MESH,
        )

    def pack(j):
        def one(w, carry):
            u = order_ref[j * deep + w]
            values = jnp.concatenate([held[a, u] for a in range(3)], axis=1)
            packed = exact_dot(pack_ref[...], values)
            for a in range(3):
                piece = packed[:, a * UNIT : (a + 1) * UNIT]
                arrive[j][w, a, pl.ds(pl.multiple_of(me_dp * room, 8), room), :] = piece[:room]
                for k in range(1, dp):
                    leave[j % 2, k - 1, w, a] = piece[k * room : (k + 1) * room]
            return carry

        lax.fori_loop(0, count(j), one, 0)
        for k in range(1, dp):
            row_copy(j, k).start()

    def unit_copy(j, k):
        peer = lax.rem(me_mp + k, mp)
        return pltpu.make_async_remote_copy(
            src_ref=unit_leave.at[j % 2, k],
            dst_ref=out_ref.at[j * mp + me_mp],
            send_sem=unit_send.at[j % 2, k],
            recv_sem=unit_recv.at[j, k],
            device_id=(me_dp, peer),
            device_id_type=MESH,
        )

    def own_copy(j):
        return pltpu.make_async_copy(
            unit_leave.at[j % 2, 0], out_ref.at[j * mp + me_mp], own_sem.at[j % 2]
        )

    def unpack(j):
        def one(k, carry):
            peer = lax.rem(me_mp + k, mp)
            w = chosen_ref[j * mp + peer]
            values = jnp.concatenate([arrive[j][w, a] for a in range(3)], axis=1)
            placed = exact_dot(take_ref[...], values)
            for a in range(3):
                unit_leave[j % 2, k, a] = placed[:, a * UNIT : (a + 1) * UNIT]
            return carry

        lax.fori_loop(0, mp, one, 0)
        for k in range(1, mp):
            unit_copy(j, k).start()
        own_copy(j).start()

    def wait_unit_send(j):
        for k in range(1, mp):
            unit_copy(j, k).wait_send()
        own_copy(j).wait()

    for a in range(3):
        pltpu.make_async_copy(held.at[a], held.at[a], load_sem.at[a]).wait()
    for j in range(min(2, chunks)):
        pack(j)
    for j in range(chunks):
        for k in range(1, dp):
            row_copy(j, k).wait_send()
        if j + 2 < chunks:
            pack(j + 2)
        for k in range(1, dp):
            row_copy(j, k).wait_recv()
        if j >= 2:
            wait_unit_send(j - 2)
        unpack(j)
    for j in range(max(chunks - 2, 0), chunks):
        wait_unit_send(j)
    for j in range(chunks):
        for k in range(1, mp):
            unit_copy(j, k).wait_recv()


def move(order, chosen, pack, take, states, dp, mp, rows, units, room, chunks):
    deep = -(-units // chunks)
    vmem = pl.BlockSpec(memory_space=pltpu.VMEM)
    smem = pl.BlockSpec(memory_space=pltpu.SMEM)
    f32 = jnp.float32
    return pl.pallas_call(
        functools.partial(move_kernel, dp, mp, rows, units, room, chunks),
        out_shape=jax.ShapeDtypeStruct((chunks * mp, 3, rows, UNIT), f32),
        in_specs=[smem, smem, vmem, vmem] + [pl.BlockSpec(memory_space=pl.ANY)] * 3,
        out_specs=pl.BlockSpec(memory_space=pl.ANY),
        scratch_shapes=[pltpu.VMEM((deep, 3, dp * room, UNIT), f32) for _ in range(chunks)]
        + [
            pltpu.VMEM((3, units, rows, UNIT), f32),
            pltpu.VMEM((2, dp - 1, deep, 3, room, UNIT), f32),
            pltpu.VMEM((2, mp, 3, rows, UNIT), f32),
            pltpu.SemaphoreType.DMA((3,)),
            pltpu.SemaphoreType.DMA((2, dp - 1)),
            pltpu.SemaphoreType.DMA((chunks, dp - 1)),
            pltpu.SemaphoreType.DMA((2, mp)),
            pltpu.SemaphoreType.DMA((chunks, mp)),
            pltpu.SemaphoreType.DMA((2,)),
        ],
        compiler_params=pltpu.CompilerParams(
            collective_id=0, has_side_effects=True, vmem_limit_bytes=60 * 2**20
        ),
    )(order, chosen, pack, take, *states)


def adam_kernel(group, landed_ref, fix_ref, *refs):
    moved = refs[:group]
    gradient_ref = refs[group]
    weight_out, first_out, second_out, update_out = refs[group + 1 :]
    first_fix = fix_ref[0]
    second_fix = fix_ref[1]
    for g in range(group):
        at = slice(g * UNIT, (g + 1) * UNIT)
        weight, first, second = moved[g][0, 0], moved[g][0, 1], moved[g][0, 2]
        gradient = gradient_ref[:, at]
        new_first = beta_one * first + (1.0 - beta_one) * gradient
        new_second = beta_two * second + (1.0 - beta_two) * gradient * gradient
        update = (
            new_first / first_fix / (jnp.sqrt(new_second / second_fix) + epsilon)
            + decay_rate * weight
        )
        weight_out[:, at] = weight - learn_rate * update
        first_out[:, at] = new_first
        second_out[:, at] = new_second
        update_out[:, at] = update


def adam(landed, fixes, moved, gradient):
    rows, columns = gradient.shape
    units = columns // UNIT
    group = next(g for g in (3, 2, 1) if units % g == 0)
    wide = pl.BlockSpec((rows, group * UNIT), lambda i, landed: (0, i))
    picks = [
        pl.BlockSpec((1, 3, rows, UNIT), lambda i, landed, g=g: (landed[i * group + g], 0, 0, 0))
        for g in range(group)
    ]
    return pl.pallas_call(
        functools.partial(adam_kernel, group),
        out_shape=[jax.ShapeDtypeStruct((rows, columns), jnp.float32)] * 4,
        grid_spec=pltpu.PrefetchScalarGridSpec(
            num_scalar_prefetch=1,
            grid=(units // group,),
            in_specs=[pl.BlockSpec(memory_space=pltpu.SMEM)] + picks + [wide],
            out_specs=[wide] * 4,
        ),
        compiler_params=pltpu.CompilerParams(vmem_limit_bytes=32 * 2**20),
    )(landed, fixes, *([moved] * group), gradient)


def body(old_weight, old_first, old_second, gradient, old_rows, new_rows, new_units, step):
    dp = lax.axis_size("dp")
    mp = lax.axis_size("mp")
    rows = old_weight.shape[0]
    units = new_units.shape[1]
    room = -(-room_for(rows, dp) // 8) * 8
    chunks = room_for(units, mp)
    pack, take = row_plan(old_rows, new_rows, lax.axis_index("dp"), room)
    order, chosen, landed = unit_plan(new_units, lax.axis_index("mp"), chunks)
    moved = move(
        order,
        chosen,
        pack,
        take,
        (old_weight, old_first, old_second),
        dp,
        mp,
        rows,
        units,
        room,
        chunks,
    )
    count = step[0].astype(jnp.float32)
    fixes = jnp.stack(
        [
            1.0 - jnp.power(jnp.float32(beta_one), count),
            1.0 - jnp.power(jnp.float32(beta_two), count),
        ]
    )
    return tuple(adam(landed, fixes, moved, gradient))


def solution(mesh):
    return jax.shard_map(
        body,
        mesh=mesh,
        in_specs=(P("dp", "mp"), P("dp", "mp"), P("dp", "mp"), P("dp", "mp"), P(), P(), P(), P()),
        out_specs=(P("dp", "mp"), P("dp", "mp"), P("dp", "mp"), P("dp", "mp")),
        check_vma=False,
    )
```

time: 794 us -> 474 us (0.60); the launches traced: 779 us -> 473 us
  Pallas kernels: 0 us -> 460 us
  blocking collectives: 429 us -> 0 us
  waiting for transfers between devices: 150 us -> 0 us
  local copies, waits for them, and re-layouts: 121 us -> 4.93 us
  other arithmetic: 64.1 us -> 7.1 us
  starting transfers between devices: 12.3 us -> 0 us
    pallas_call x0 -> x2, Pallas kernels: none -> 460 us  [the longest x1 444 us: move(): pl.pallas_call(functools.partial(move_kernel, dp, mp, rows, units, room,...]
    all_to_all x4 -> x0, blocking collectives: 429 us -> none  [the longest x1 139 us: body(): lax.all_to_all(packed[1], 'dp', split_axis=0, concat_axis=0, tiled=True)]
    all_to_all x2 -> x0, waiting for transfers between devices: 150 us -> none  [the longest x1 98.9 us: body(): lax.all_to_all(packed[0], 'dp', split_axis=0, concat_axis=0, tiled=True)]
    gather x18 -> x0, local copies, waits for them, and re-layouts: 105 us -> none  [the longest x3 35.8 us: body(): jnp.take(moment, row_send, axis=0, mode='fill', fill_value=0)]
    select_n x11 -> x2, other arithmetic: 20.5 us -> 0.02 us  [the longest x1 0.01 us: unit_plan(): iota(total) // per]
    sort x4 -> x0, other arithmetic: 16.2 us -> none  [the longest x2 8.15 us: moving_plan(): new_place = jnp.argsort(new_flat, stable=True)]
    unnamed x2 -> x0, other arithmetic: 14.4 us -> none
    reshape x9 -> x2, local copies, waits for them, and re-layouts: 14.1 us -> 0.15 us  [the longest x1 0.08 us: row_plan(): jnp.sum(same * (iota(total) // per)[None, :], axis=1).reshape(shards, per)]
  transfers between devices with their start and end apart: 2 -> 0, of which waited for: 2 -> 0; matrix products, arithmetic and copies ran while one was open for 6% -> 0% of each run, Pallas kernels for 0% -> 0%
where the time goes in v1:
time: 474 us; the launch traced here: 473 us
  Pallas kernels  460 us (97%)
  other arithmetic  7.1 us (1%)
  local copies, waits for them, and re-layouts  4.93 us (1%)
    pallas_call x1, Pallas kernels, move(): pl.pallas_call(functools.partial(move_kernel, dp, mp, rows, units, room,...  444 us
    pallas_call x1, Pallas kernels, adam(): pl.pallas_call(functools.partial(adam_kernel, group), out_shape=[jax.Shap...  16 us

profile of v1, /device:TPU:9, one launch (start us, length us, event | category | flops | bytes accessed | tf_op | source)
XLA Modules:
  0.0 473.2 jit_solution(6991180085432723519)
XLA Ops:
  1.4 0.6 pad_maximum_fusion.fix_ref
  2.0 0.7 fusion.22
  2.6 0.8 eq.151
  3.4 0.2 select_reduce_fusion.2
  3.8 0.8 eq.164
  4.5 0.8 eq.166
  5.3 0.4 select_reduce_fusion
  5.8 0.1 add.100
  5.9 0.1 copy.13
  6.0 0.9 convert_reduce_fusion.1
  6.8 0.2 fusion.4
  7.1 0.1 reduce_sum.76
  7.2 0.7 select_reduce_fusion.3.landed_ref
  7.9 0.7 select_reduce_fusion.5.refs_0_
  8.6 0.6 select_reduce_fusion.4.refs_1_
  9.3 0.4 convert_reduce_fusion
  9.7 0.7 constant_dynamic-slice_fusion.1
  10.5 0.2 select_reduce_fusion.1
  10.7 0.7 fusion.refs_2_
  11.4 0.8 fusion.1.refs_3_
  12.1 443.7 %shard_map.111.refs_0_.refs_1_.refs_2_ = f32[64,3,192,128]{3,2,1,0:T(8,128)} custom-call(s32[48]{0:T(128)} %select_reduce_fusion.5.refs_0_, s32[64]{0:T(128)} %select_reduce_fusion.4.refs_1_, bf16[288,192]{1,0:T(8,128)(2,1)} %fusion.refs_2_, bf16[192,288]{1,0:T(8,128)(2,1)} %fusion.1.refs_3_, f32[192,5376]{1,0:T(8,128)} %refs_4_.1, f32[192,5376]{1,0:T(8,128)} %refs_5_.1, ...), custom_call_target="tpu_custom_call" | custom-call | tf_op jit(solution)/shard_map/pallas_call | solution.py:215
  455.9 0.6 copy-done.1
  456.6 0.7 copy-done.2
  457.2 16.0 %shard_map.112 = (f32[192,5376]{1,0:T(8,128)}, f32[192,5376]{1,0:T(8,128)}, f32[192,5376]{1,0:T(8,128)}, f32[192,5376]{1,0:T(8,128)}) custom-call(s32[42]{0:T(128)S(1)} %copy-done.1, f32[2]{0:T(128)S(1)} %copy-done.2, f32[64,3,192,128]{3,2,1,0:T(8,128)} %shard_map.111.refs_0_.refs_1_.refs_2_, f32[64,3,192,128]{3,2,1,0:T(8,128)} %shard_map.111.refs_0_.refs_1_.refs_2_, ...), custom_call_target="tpu_custom_call" | custom-call | tf_op jit(solution)/shard_map/pallas_call | solution.py:269
  (18 shorter events, 0.5 us)
Async XLA Ops:
  12.1 443.8 %copy-start = (f32[192,5376]{1,0:T(8,128)S(1)}, f32[192,5376]{1,0:T(8,128)}, u32[]{:S(2)}) copy-start(f32[192,5376]{1,0:T(8,128)} %refs_3_.1) | copy-start | bytes 12386308
  455.9 0.7 copy-start.1
  456.6 0.7 copy-start.2
